TPU v7x, 512 devices: a whole 4x4x16 slice. The times are simulated.
512 devices in a mesh: segment: 8 (over y, core), rows: 16 (over z), dp: 4 (over x).
Axes of the slice: x: 4, y: 4, z: 16, core: 2. Of those that a mesh axis runs over, the one named last changes fastest.
Arguments:
- clips: bfloat16 [4, 4, 4, 128, 8, 128], P(None, 'dp', None, 'rows'), may hold values from -80 to 80
- lengths: int32 [4, 4], P(None, 'dp'), may hold values from 1 to 4, as said below
- conv_weight: bfloat16 [8, 3456, 128], P('segment'), may hold values from -0.109375 to 0.109375
- norm_gain: float32 [8, 128], P('segment'), may hold values from 0.5 to 2
- norm_shift: float32 [8, 128], P('segment'), may hold values from -1 to 1
- conv_bias: float32 [8, 128], P('segment'), may hold values from -3 to 3
- cotangent: bfloat16 [8, 4, 4, 4, 128, 8, 128], P('segment', None, 'dp', None, 'rows'), may hold values from -6 to 6
Outputs:
- stash: bfloat16 [8, 4, 4, 4, 128, 8, 128], P('segment', None, 'dp', None, 'rows')
- weight_grad: float32 [8, 3456, 128], P('segment')
Inputs may be any that keep to these rules, and one draw needn't show every extreme that they name: lengths[m, clip] real frames lead each clip; the frames after them are padding; some clip has all 4 frames.
All inputs are finite; a program needn't handle non-finite values.
Results may differ from a plain program's by a relative error of at most 0.009.
Values may be sent and summed in bfloat16 or wider, within the bound.
A program may use at most 64 MiB of HBM per device.

v0:
```python
import math
import jax
import jax.numpy as jnp
from jax import lax
from jax.sharding import PartitionSpec as P

GROUPS = 32
eps = 1e-06


def extended_2(cells, sides, width):
    for axis, dim in sides:
        count = lax.axis_size(axis)
        ends = count - 1
        head = lax.slice_in_dim(cells, 0, width, axis=dim)
        tail = lax.slice_in_dim(cells, cells.shape[dim] - width, cells.shape[dim], axis=dim)
        cells = jnp.concatenate(
            [
                lax.ppermute(tail, axis, [(i, (i + 1) % count) for i in range(ends)]),
                cells,
                lax.ppermute(head, axis, [((i + 1) % count, i) for i in range(ends)]),
            ],
            axis=dim,
        )
    return cells


def passed_along(block, axis, distance):
    devices = range(lax.axis_size(axis))
    route = [(i - distance, i) for i in devices if i - distance in devices]
    return lax.ppermute(block, axis, route)


def statistics(values, frame_mask, length, height):
    clip_count, frames, rows_here, cols, chans = values.shape
    sub = chans // GROUPS
    grouped = values.reshape(clip_count, frames, rows_here, cols, GROUPS, sub)
    mask_six = frame_mask[:, :, :, :, :, None]
    count = (length * (height * cols * sub)).astype(jnp.float32)[:, None]
    total = lax.psum(jnp.sum(grouped * mask_six, axis=(1, 2, 3, 5)), "rows")
    mean = total / count
    centered = grouped - mean[:, None, None, None, :, None]
    spread = lax.psum(jnp.sum(centered * centered * mask_six, axis=(1, 2, 3, 5)), "rows")
    var = spread / count
    rstd = lax.rsqrt(var + eps)
    mean_chan = jnp.repeat(mean, sub, axis=-1)[:, None, None, None, :]
    rstd_chan = jnp.repeat(rstd, sub, axis=-1)[:, None, None, None, :]
    return (mean_chan, rstd_chan)


def block(current, length, weight, gain, shift, bias, height):
    clip_count, frames, rows_here, cols, chans = current.shape
    values = current.astype(jnp.float32)
    frame_mask = (jnp.arange(frames)[None, :] < length[:, None]).astype(jnp.float32)[
        :, :, None, None, None
    ]
    mean_chan, rstd_chan = statistics(values, frame_mask, length, height)
    hidden = jax.nn.silu((values - mean_chan) * rstd_chan * gain + shift).astype(jnp.bfloat16)
    extended = extended_2(hidden, (("rows", 2),), 1)
    padded = jnp.pad(extended, ((0, 0), (0, 0), (0, 0), (1, 1), (0, 0)))
    padded = jnp.concatenate([padded[:, :1], padded[:, :1], padded], axis=1)
    pieces = []
    for tap_t in range(3):
        for tap_h in range(3):
            for tap_w in range(3):
                pieces.append(
                    padded[
                        :,
                        tap_t : tap_t + frames,
                        tap_h : tap_h + rows_here,
                        tap_w : tap_w + cols,
                        :,
                    ]
                )
    patches = jnp.concatenate(pieces, axis=-1).reshape(-1, 27 * chans)
    conv = jnp.dot(patches, weight, preferred_element_type=jnp.float32).reshape(values.shape)
    result = ((values + conv + bias) * frame_mask).astype(jnp.bfloat16)
    return (result, patches, frame_mask.astype(jnp.bfloat16))


def per_device(clips, lengths, conv_weight, norm_gain, norm_shift, conv_bias, cotangent):
    segments = lax.axis_size("segment")
    segment_id = lax.axis_index("segment")
    micro = clips.shape[0]
    frames = clips.shape[2]
    cols = clips.shape[4]
    chans = clips.shape[5]
    height = clips.shape[3] * lax.axis_size("rows")
    weight = conv_weight[0]
    gain = norm_gain[0]
    shift = norm_shift[0]
    bias = conv_bias[0]
    cot_all = cotangent[0]
    total_cells = micro * clips.shape[1] * lax.axis_size("dp") * frames * height * cols
    factor = 1.0 / math.sqrt(total_cells)

    def tick(step, carry):
        arrived, stash, grads = carry
        which = step - segment_id
        valid = (which >= 0) & (which < micro)
        slot = jnp.clip(which, 0, micro - 1)
        fresh = lax.dynamic_index_in_dim(
            clips, jnp.clip(step, 0, micro - 1).astype(jnp.int32), 0, keepdims=False
        )
        current = jnp.where(segment_id == 0, fresh, arrived)
        length = lax.dynamic_index_in_dim(lengths, slot, 0, keepdims=False)
        result, patches, mask_five = block(current, length, weight, gain, shift, bias, height)
        cot_now = lax.dynamic_index_in_dim(cot_all, slot, 0, keepdims=False)
        masked = (cot_now * mask_five).reshape(-1, chans)
        term = lax.dot_general(
            patches, masked, (((0,), (0,)), ((), ())), preferred_element_type=jnp.float32
        )
        grads = grads + jnp.where(valid, term, 0.0)
        previous = lax.dynamic_index_in_dim(stash, slot, 0, keepdims=False)
        stash = lax.dynamic_update_index_in_dim(stash, jnp.where(valid, result, previous), slot, 0)
        arrived = passed_along(result, "segment", 1)
        return (arrived, stash, grads)

    start = (
        jnp.zeros(clips.shape[1:], jnp.bfloat16),
        jnp.zeros(clips.shape, jnp.bfloat16),
        jnp.zeros((27 * chans, chans), jnp.float32),
    )
    arrived, stash, grads = lax.fori_loop(0, micro + segments - 1, tick, start)
    grads = lax.psum(grads, ("rows", "dp")) * factor
    return (stash[None], grads[None])


def solution(mesh):
    in_specs = (
        P(None, "dp", None, "rows", None, None),
        P(None, "dp"),
        P("segment", None, None),
        P("segment", None),
        P("segment", None),
        P("segment", None),
        P("segment", None, "dp", None, "rows", None, None),
    )
    out_specs = (P("segment", None, "dp", None, "rows", None, None), P("segment", None, None))
    return jax.shard_map(
        per_device, mesh=mesh, in_specs=in_specs, out_specs=out_specs, check_vma=False
    )
```

profile of v0, /device:TPU:8, one launch (start us, length us, event | category | flops | bytes accessed | tf_op | source)
XLA Modules:
  0.0 1160.9 jit_solution(13718055022507466365)
XLA Ops:
  7.3 867.2 %while.20 = (s32[]{:T(128)}, bf16[1,4,8,8,128]{4,3,2,1,0:T(8,128)(2,1)S(1)}, bf16[4,1,4,8,8,128]{5,4,3,2,1,0:T(8,128)(2,1)S(1)}, f32[3456,128]{1,0:T(8,128)S(1)}...) while((s32[]{:T(128)}, ...), condition=%wide.region_7.8_spmd.clone, body=%wide.region_0.7_spmd.clone.sunk | while | flops 457701504 | bytes 18060908 | solution.py:124
  10.4 36.5 %psum.40 = f32[1,32]{1,0:T(1,128)S(1)} all-reduce(f32[1,32]{1,0:T(1,128)S(1)} %bitcast.110), channel_id=1, replica_groups=mesh['segment'=8,'rows'=16,'dp'=4] {'rows'}, use_global_device_ids=true, to_apply=%region_3.3 | all-reduce | flops 32 | bytes 256 | tf_op jit(solution)/shard_map/while/body/eval_jaxpr/psum | solution.py:40
  48.0 27.0 %psum.41 = f32[1,32]{1,0:T(1,128)S(1)} all-reduce(f32[1,32]{1,0:T(1,128)S(1)} %bitcast.109), channel_id=1, replica_groups=mesh['segment'=8,'rows'=16,'dp'=4] {'rows'}, use_global_device_ids=true, to_apply=%region_6.6 | all-reduce | flops 32 | bytes 256 | tf_op jit(solution)/shard_map/while/body/eval_jaxpr/psum | solution.py:43
  77.3 4.5 collective-permute-start.1
  94.2 30.5 %psum.40 = f32[1,32]{1,0:T(1,128)S(1)} all-reduce(f32[1,32]{1,0:T(1,128)S(1)} %bitcast.110), channel_id=1, replica_groups=mesh['segment'=8,'rows'=16,'dp'=4] {'rows'}, use_global_device_ids=true, to_apply=%region_3.3 | all-reduce | flops 32 | bytes 256 | tf_op jit(solution)/shard_map/while/body/eval_jaxpr/psum | solution.py:40
  125.8 29.1 %psum.41 = f32[1,32]{1,0:T(1,128)S(1)} all-reduce(f32[1,32]{1,0:T(1,128)S(1)} %bitcast.109), channel_id=1, replica_groups=mesh['segment'=8,'rows'=16,'dp'=4] {'rows'}, use_global_device_ids=true, to_apply=%region_6.6 | all-reduce | flops 32 | bytes 256 | tf_op jit(solution)/shard_map/while/body/eval_jaxpr/psum | solution.py:43
  157.2 4.5 collective-permute-start.1
  174.0 29.3 %psum.40 = f32[1,32]{1,0:T(1,128)S(1)} all-reduce(f32[1,32]{1,0:T(1,128)S(1)} %bitcast.110), channel_id=1, replica_groups=mesh['segment'=8,'rows'=16,'dp'=4] {'rows'}, use_global_device_ids=true, to_apply=%region_3.3 | all-reduce | flops 32 | bytes 256 | tf_op jit(solution)/shard_map/while/body/eval_jaxpr/psum | solution.py:40
  204.5 28.3 %psum.41 = f32[1,32]{1,0:T(1,128)S(1)} all-reduce(f32[1,32]{1,0:T(1,128)S(1)} %bitcast.109), channel_id=1, replica_groups=mesh['segment'=8,'rows'=16,'dp'=4] {'rows'}, use_global_device_ids=true, to_apply=%region_6.6 | all-reduce | flops 32 | bytes 256 | tf_op jit(solution)/shard_map/while/body/eval_jaxpr/psum | solution.py:43
  235.0 4.5 collective-permute-start.1
  251.8 29.3 %psum.40 = f32[1,32]{1,0:T(1,128)S(1)} all-reduce(f32[1,32]{1,0:T(1,128)S(1)} %bitcast.110), channel_id=1, replica_groups=mesh['segment'=8,'rows'=16,'dp'=4] {'rows'}, use_global_device_ids=true, to_apply=%region_3.3 | all-reduce | flops 32 | bytes 256 | tf_op jit(solution)/shard_map/while/body/eval_jaxpr/psum | solution.py:40
  282.3 29.0 %psum.41 = f32[1,32]{1,0:T(1,128)S(1)} all-reduce(f32[1,32]{1,0:T(1,128)S(1)} %bitcast.109), channel_id=1, replica_groups=mesh['segment'=8,'rows'=16,'dp'=4] {'rows'}, use_global_device_ids=true, to_apply=%region_6.6 | all-reduce | flops 32 | bytes 256 | tf_op jit(solution)/shard_map/while/body/eval_jaxpr/psum | solution.py:43
  313.6 4.5 collective-permute-start.1
  330.4 29.3 %psum.40 = f32[1,32]{1,0:T(1,128)S(1)} all-reduce(f32[1,32]{1,0:T(1,128)S(1)} %bitcast.110), channel_id=1, replica_groups=mesh['segment'=8,'rows'=16,'dp'=4] {'rows'}, use_global_device_ids=true, to_apply=%region_3.3 | all-reduce | flops 32 | bytes 256 | tf_op jit(solution)/shard_map/while/body/eval_jaxpr/psum | solution.py:40
  360.9 28.2 %psum.41 = f32[1,32]{1,0:T(1,128)S(1)} all-reduce(f32[1,32]{1,0:T(1,128)S(1)} %bitcast.109), channel_id=1, replica_groups=mesh['segment'=8,'rows'=16,'dp'=4] {'rows'}, use_global_device_ids=true, to_apply=%region_6.6 | all-reduce | flops 32 | bytes 256 | tf_op jit(solution)/shard_map/while/body/eval_jaxpr/psum | solution.py:43
  391.4 4.5 collective-permute-start.1
  408.3 29.3 %psum.40 = f32[1,32]{1,0:T(1,128)S(1)} all-reduce(f32[1,32]{1,0:T(1,128)S(1)} %bitcast.110), channel_id=1, replica_groups=mesh['segment'=8,'rows'=16,'dp'=4] {'rows'}, use_global_device_ids=true, to_apply=%region_3.3 | all-reduce | flops 32 | bytes 256 | tf_op jit(solution)/shard_map/while/body/eval_jaxpr/psum | solution.py:40
  438.8 29.0 %psum.41 = f32[1,32]{1,0:T(1,128)S(1)} all-reduce(f32[1,32]{1,0:T(1,128)S(1)} %bitcast.109), channel_id=1, replica_groups=mesh['segment'=8,'rows'=16,'dp'=4] {'rows'}, use_global_device_ids=true, to_apply=%region_6.6 | all-reduce | flops 32 | bytes 256 | tf_op jit(solution)/shard_map/while/body/eval_jaxpr/psum | solution.py:43
  470.0 4.5 collective-permute-start.1
  486.9 29.3 %psum.40 = f32[1,32]{1,0:T(1,128)S(1)} all-reduce(f32[1,32]{1,0:T(1,128)S(1)} %bitcast.110), channel_id=1, replica_groups=mesh['segment'=8,'rows'=16,'dp'=4] {'rows'}, use_global_device_ids=true, to_apply=%region_3.3 | all-reduce | flops 32 | bytes 256 | tf_op jit(solution)/shard_map/while/body/eval_jaxpr/psum | solution.py:40
  517.4 28.2 %psum.41 = f32[1,32]{1,0:T(1,128)S(1)} all-reduce(f32[1,32]{1,0:T(1,128)S(1)} %bitcast.109), channel_id=1, replica_groups=mesh['segment'=8,'rows'=16,'dp'=4] {'rows'}, use_global_device_ids=true, to_apply=%region_6.6 | all-reduce | flops 32 | bytes 256 | tf_op jit(solution)/shard_map/while/body/eval_jaxpr/psum | solution.py:43
  564.7 29.3 %psum.40 = f32[1,32]{1,0:T(1,128)S(1)} all-reduce(f32[1,32]{1,0:T(1,128)S(1)} %bitcast.110), channel_id=1, replica_groups=mesh['segment'=8,'rows'=16,'dp'=4] {'rows'}, use_global_device_ids=true, to_apply=%region_3.3 | all-reduce | flops 32 | bytes 256 | tf_op jit(solution)/shard_map/while/body/eval_jaxpr/psum | solution.py:40
  595.2 29.0 %psum.41 = f32[1,32]{1,0:T(1,128)S(1)} all-reduce(f32[1,32]{1,0:T(1,128)S(1)} %bitcast.109), channel_id=1, replica_groups=mesh['segment'=8,'rows'=16,'dp'=4] {'rows'}, use_global_device_ids=true, to_apply=%region_6.6 | all-reduce | flops 32 | bytes 256 | tf_op jit(solution)/shard_map/while/body/eval_jaxpr/psum | solution.py:43
  626.5 4.5 collective-permute-start.1
  643.3 29.3 %psum.40 = f32[1,32]{1,0:T(1,128)S(1)} all-reduce(f32[1,32]{1,0:T(1,128)S(1)} %bitcast.110), channel_id=1, replica_groups=mesh['segment'=8,'rows'=16,'dp'=4] {'rows'}, use_global_device_ids=true, to_apply=%region_3.3 | all-reduce | flops 32 | bytes 256 | tf_op jit(solution)/shard_map/while/body/eval_jaxpr/psum | solution.py:40
  673.8 28.2 %psum.41 = f32[1,32]{1,0:T(1,128)S(1)} all-reduce(f32[1,32]{1,0:T(1,128)S(1)} %bitcast.109), channel_id=1, replica_groups=mesh['segment'=8,'rows'=16,'dp'=4] {'rows'}, use_global_device_ids=true, to_apply=%region_6.6 | all-reduce | flops 32 | bytes 256 | tf_op jit(solution)/shard_map/while/body/eval_jaxpr/psum | solution.py:43
  704.3 4.5 collective-permute-start.1
  721.1 29.3 %psum.40 = f32[1,32]{1,0:T(1,128)S(1)} all-reduce(f32[1,32]{1,0:T(1,128)S(1)} %bitcast.110), channel_id=1, replica_groups=mesh['segment'=8,'rows'=16,'dp'=4] {'rows'}, use_global_device_ids=true, to_apply=%region_3.3 | all-reduce | flops 32 | bytes 256 | tf_op jit(solution)/shard_map/while/body/eval_jaxpr/psum | solution.py:40
  751.6 29.0 %psum.41 = f32[1,32]{1,0:T(1,128)S(1)} all-reduce(f32[1,32]{1,0:T(1,128)S(1)} %bitcast.109), channel_id=1, replica_groups=mesh['segment'=8,'rows'=16,'dp'=4] {'rows'}, use_global_device_ids=true, to_apply=%region_6.6 | all-reduce | flops 32 | bytes 256 | tf_op jit(solution)/shard_map/while/body/eval_jaxpr/psum | solution.py:43
  799.7 29.3 %psum.40 = f32[1,32]{1,0:T(1,128)S(1)} all-reduce(f32[1,32]{1,0:T(1,128)S(1)} %bitcast.110), channel_id=1, replica_groups=mesh['segment'=8,'rows'=16,'dp'=4] {'rows'}, use_global_device_ids=true, to_apply=%region_3.3 | all-reduce | flops 32 | bytes 256 | tf_op jit(solution)/shard_map/while/body/eval_jaxpr/psum | solution.py:40
  830.2 28.2 %psum.41 = f32[1,32]{1,0:T(1,128)S(1)} all-reduce(f32[1,32]{1,0:T(1,128)S(1)} %bitcast.109), channel_id=1, replica_groups=mesh['segment'=8,'rows'=16,'dp'=4] {'rows'}, use_global_device_ids=true, to_apply=%region_6.6 | all-reduce | flops 32 | bytes 256 | tf_op jit(solution)/shard_map/while/body/eval_jaxpr/psum | solution.py:43
  875.8 275.4 %all-reduce.3.cloned.1.call-done = f32[3456,128]{1,0:T(8,128)} async-done(((f32[3456,128]{1,0:T(8,128)}), f32[3456,128]{1,0:T(8,128)}) %all-reduce.3.cloned.1.call-update) | async-done | bytes 1769488 | tf_op jit(solution)/shard_map/psum | solution.py:125
  (706 shorter events, 180.5 us)
Async XLA Ops:
  7.2 1144.0 %all-reduce.3.cloned.1.call-start = ((), (), s32[]{:S(2)}) async-start(), calls=%async_computation | async-start | bytes 3538944 | tf_op jit(solution)/shard_map/psum | solution.py:125
  76.0 6.5 collective-permute-start
  77.3 5.9 collective-permute-start.1
  85.6 5.6 collective-permute-start.2
  155.9 6.5 collective-permute-start
  157.2 5.9 collective-permute-start.1
  165.4 5.6 collective-permute-start.2
  233.7 6.5 collective-permute-start
  235.0 5.9 collective-permute-start.1
  243.2 5.6 collective-permute-start.2
  312.3 6.5 collective-permute-start
  313.6 5.9 collective-permute-start.1
  321.8 5.6 collective-permute-start.2
  390.1 6.5 collective-permute-start
  391.4 5.9 collective-permute-start.1
  399.7 5.6 collective-permute-start.2
  468.7 6.5 collective-permute-start
  470.0 5.9 collective-permute-start.1
  478.3 5.6 collective-permute-start.2
  546.6 6.5 collective-permute-start
  547.9 5.9 collective-permute-start.1
  556.1 5.6 collective-permute-start.2
  625.2 6.5 collective-permute-start
  626.5 5.9 collective-permute-start.1
  634.7 5.6 collective-permute-start.2
  703.0 6.5 collective-permute-start
  704.3 5.9 collective-permute-start.1
  712.5 5.6 collective-permute-start.2
  781.6 6.5 collective-permute-start
  782.9 5.9 collective-permute-start.1
  859.4 6.5 collective-permute-start
  860.7 5.9 collective-permute-start.1
  (48 other events, 333.2 us)
Sparse Core Ops, SparseCore 0:
  875.9 275.2 all-reduce.2
where the time goes:
time: 1160 us
  blocking collectives  644 us (56%)
  waiting for transfers between devices  299 us (26%)
  starting transfers between devices  85.4 us (7%)
  other arithmetic  58.3 us (5%)
  matrix products  32.1 us (3%)
  local copies, waits for them, and re-layouts  17.7 us (2%)
  between operations  14.1 us (1%)
    psum x11, blocking collectives, statistics(): total = lax.psum(jnp.sum(grouped * mask_six, axis=(1, 2, 3, 5)), 'rows')  331 us
    psum x11, blocking collectives, statistics(): lax.psum(jnp.sum(centered * centered * mask_six, axis=(1, 2, 3, 5)), 'rows')  313 us
    psum x1, waiting for transfers between devices, per_device(): grads = lax.psum(grads, ('rows', 'dp')) * factor  275 us
    ppermute x11, starting transfers between devices, extended_2(): lax.ppermute(tail, axis, [(i, (i + 1) % count) for i in range(ends)])  50 us
    dot_general x11, matrix products, tick(): lax.dot_general(patches, masked, (((0,), (0,)), ((), ())), preferred_elem...  24.9 us
  transfers between devices with their start and end apart: 34, of which 23 were waited for; matrix products, arithmetic and copies ran while one was open for 3% of the time, Pallas kernels for 0%

commit v1 on v0

--- a/solution.py
+++ b/solution.py
@@ -122,7 +122,7 @@
         jnp.zeros((27 * chans, chans), jnp.float32),
     )
     arrived, stash, grads = lax.fori_loop(0, micro + segments - 1, tick, start)
-    grads = lax.psum(grads, ("rows", "dp")) * factor
+    grads = lax.psum(lax.psum(grads, "dp"), "rows") * factor
     return (stash[None], grads[None])
 
 

time: 1160 us -> 1100 us (0.948)
  the two profiles are of different devices: /device:TPU:8 before, /device:TPU:2 now
where the time goes in v1:
time: 1100 us
  blocking collectives  643 us (58%)
  waiting for transfers between devices  236 us (21%)
  starting transfers between devices  84.6 us (8%)
  other arithmetic  58.4 us (5%)
  matrix products  32.1 us (3%)
  local copies, waits for them, and re-layouts  17.7 us (2%)
  between operations  14.1 us (1%)
    psum x11, blocking collectives, statistics(): total = lax.psum(jnp.sum(grouped * mask_six, axis=(1, 2, 3, 5)), 'rows')  330 us
    psum x11, blocking collectives, statistics(): lax.psum(jnp.sum(centered * centered * mask_six, axis=(1, 2, 3, 5)), 'rows')  313 us
    psum x2, waiting for transfers between devices, per_device(): grads = lax.psum(lax.psum(grads, 'dp'), 'rows') * factor  228 us
    ppermute x11, starting transfers between devices, extended_2(): lax.ppermute(tail, axis, [(i, (i + 1) % count) for i in range(ends)])  50 us
    dot_general x11, matrix products, tick(): lax.dot_general(patches, masked, (((0,), (0,)), ((), ())), preferred_elem...  24.9 us
  transfers between devices with their start and end apart: 35, of which 13 were waited for; matrix products, arithmetic and copies ran while one was open for 3% of the time, Pallas kernels for 0%

profile of v1, /device:TPU:2, one launch (start us, length us, event | category | flops | bytes accessed | tf_op | source)
XLA Modules:
  0.0 1097.5 jit_solution(11393954254351184470)
XLA Ops:
  7.3 850.9 %while.20 = (s32[]{:T(128)}, bf16[1,4,8,8,128]{4,3,2,1,0:T(8,128)(2,1)S(1)}, bf16[4,1,4,8,8,128]{5,4,3,2,1,0:T(8,128)(2,1)S(1)}, f32[3456,128]{1,0:T(8,128)S(1)}...) while((s32[]{:T(128)}, ...), condition=%wide.region_7.8_spmd.clone, body=%wide.region_0.7_spmd.clone.sunk | while | flops 457701504 | bytes 18060908 | solution.py:124
  10.4 36.5 %psum.48 = f32[1,32]{1,0:T(1,128)S(1)} all-reduce(f32[1,32]{1,0:T(1,128)S(1)} %bitcast.110), channel_id=1, replica_groups=mesh['segment'=8,'rows'=16,'dp'=4] {'rows'}, use_global_device_ids=true, to_apply=%region_3.3 | all-reduce | flops 32 | bytes 256 | tf_op jit(solution)/shard_map/while/body/eval_jaxpr/psum | solution.py:40
  48.0 27.0 %psum.49 = f32[1,32]{1,0:T(1,128)S(1)} all-reduce(f32[1,32]{1,0:T(1,128)S(1)} %bitcast.109), channel_id=1, replica_groups=mesh['segment'=8,'rows'=16,'dp'=4] {'rows'}, use_global_device_ids=true, to_apply=%region_6.6 | all-reduce | flops 32 | bytes 256 | tf_op jit(solution)/shard_map/while/body/eval_jaxpr/psum | solution.py:43
  92.2 30.5 %psum.48 = f32[1,32]{1,0:T(1,128)S(1)} all-reduce(f32[1,32]{1,0:T(1,128)S(1)} %bitcast.110), channel_id=1, replica_groups=mesh['segment'=8,'rows'=16,'dp'=4] {'rows'}, use_global_device_ids=true, to_apply=%region_3.3 | all-reduce | flops 32 | bytes 256 | tf_op jit(solution)/shard_map/while/body/eval_jaxpr/psum | solution.py:40
  123.9 29.0 %psum.49 = f32[1,32]{1,0:T(1,128)S(1)} all-reduce(f32[1,32]{1,0:T(1,128)S(1)} %bitcast.109), channel_id=1, replica_groups=mesh['segment'=8,'rows'=16,'dp'=4] {'rows'}, use_global_device_ids=true, to_apply=%region_6.6 | all-reduce | flops 32 | bytes 256 | tf_op jit(solution)/shard_map/while/body/eval_jaxpr/psum | solution.py:43
  155.1 4.5 collective-permute-start.1
  170.0 29.3 %psum.48 = f32[1,32]{1,0:T(1,128)S(1)} all-reduce(f32[1,32]{1,0:T(1,128)S(1)} %bitcast.110), channel_id=1, replica_groups=mesh['segment'=8,'rows'=16,'dp'=4] {'rows'}, use_global_device_ids=true, to_apply=%region_3.3 | all-reduce | flops 32 | bytes 256 | tf_op jit(solution)/shard_map/while/body/eval_jaxpr/psum | solution.py:40
  200.5 28.3 %psum.49 = f32[1,32]{1,0:T(1,128)S(1)} all-reduce(f32[1,32]{1,0:T(1,128)S(1)} %bitcast.109), channel_id=1, replica_groups=mesh['segment'=8,'rows'=16,'dp'=4] {'rows'}, use_global_device_ids=true, to_apply=%region_6.6 | all-reduce | flops 32 | bytes 256 | tf_op jit(solution)/shard_map/while/body/eval_jaxpr/psum | solution.py:43
  231.1 4.5 collective-permute-start.1
  245.9 29.3 %psum.48 = f32[1,32]{1,0:T(1,128)S(1)} all-reduce(f32[1,32]{1,0:T(1,128)S(1)} %bitcast.110), channel_id=1, replica_groups=mesh['segment'=8,'rows'=16,'dp'=4] {'rows'}, use_global_device_ids=true, to_apply=%region_3.3 | all-reduce | flops 32 | bytes 256 | tf_op jit(solution)/shard_map/while/body/eval_jaxpr/psum | solution.py:40
  276.5 28.9 %psum.49 = f32[1,32]{1,0:T(1,128)S(1)} all-reduce(f32[1,32]{1,0:T(1,128)S(1)} %bitcast.109), channel_id=1, replica_groups=mesh['segment'=8,'rows'=16,'dp'=4] {'rows'}, use_global_device_ids=true, to_apply=%region_6.6 | all-reduce | flops 32 | bytes 256 | tf_op jit(solution)/shard_map/while/body/eval_jaxpr/psum | solution.py:43
  307.6 4.5 collective-permute-start.1
  322.5 29.3 %psum.48 = f32[1,32]{1,0:T(1,128)S(1)} all-reduce(f32[1,32]{1,0:T(1,128)S(1)} %bitcast.110), channel_id=1, replica_groups=mesh['segment'=8,'rows'=16,'dp'=4] {'rows'}, use_global_device_ids=true, to_apply=%region_3.3 | all-reduce | flops 32 | bytes 256 | tf_op jit(solution)/shard_map/while/body/eval_jaxpr/psum | solution.py:40
  353.0 28.3 %psum.49 = f32[1,32]{1,0:T(1,128)S(1)} all-reduce(f32[1,32]{1,0:T(1,128)S(1)} %bitcast.109), channel_id=1, replica_groups=mesh['segment'=8,'rows'=16,'dp'=4] {'rows'}, use_global_device_ids=true, to_apply=%region_6.6 | all-reduce | flops 32 | bytes 256 | tf_op jit(solution)/shard_map/while/body/eval_jaxpr/psum | solution.py:43
  383.6 4.5 collective-permute-start.1
  398.4 29.3 %psum.48 = f32[1,32]{1,0:T(1,128)S(1)} all-reduce(f32[1,32]{1,0:T(1,128)S(1)} %bitcast.110), channel_id=1, replica_groups=mesh['segment'=8,'rows'=16,'dp'=4] {'rows'}, use_global_device_ids=true, to_apply=%region_3.3 | all-reduce | flops 32 | bytes 256 | tf_op jit(solution)/shard_map/while/body/eval_jaxpr/psum | solution.py:40
  428.9 29.0 %psum.49 = f32[1,32]{1,0:T(1,128)S(1)} all-reduce(f32[1,32]{1,0:T(1,128)S(1)} %bitcast.109), channel_id=1, replica_groups=mesh['segment'=8,'rows'=16,'dp'=4] {'rows'}, use_global_device_ids=true, to_apply=%region_6.6 | all-reduce | flops 32 | bytes 256 | tf_op jit(solution)/shard_map/while/body/eval_jaxpr/psum | solution.py:43
  460.2 4.5 collective-permute-start.1
  475.1 29.3 %psum.48 = f32[1,32]{1,0:T(1,128)S(1)} all-reduce(f32[1,32]{1,0:T(1,128)S(1)} %bitcast.110), channel_id=1, replica_groups=mesh['segment'=8,'rows'=16,'dp'=4] {'rows'}, use_global_device_ids=true, to_apply=%region_3.3 | all-reduce | flops 32 | bytes 256 | tf_op jit(solution)/shard_map/while/body/eval_jaxpr/psum | solution.py:40
  505.6 28.2 %psum.49 = f32[1,32]{1,0:T(1,128)S(1)} all-reduce(f32[1,32]{1,0:T(1,128)S(1)} %bitcast.109), channel_id=1, replica_groups=mesh['segment'=8,'rows'=16,'dp'=4] {'rows'}, use_global_device_ids=true, to_apply=%region_6.6 | all-reduce | flops 32 | bytes 256 | tf_op jit(solution)/shard_map/while/body/eval_jaxpr/psum | solution.py:43
  536.1 4.5 collective-permute-start.1
  551.0 29.3 %psum.48 = f32[1,32]{1,0:T(1,128)S(1)} all-reduce(f32[1,32]{1,0:T(1,128)S(1)} %bitcast.110), channel_id=1, replica_groups=mesh['segment'=8,'rows'=16,'dp'=4] {'rows'}, use_global_device_ids=true, to_apply=%region_3.3 | all-reduce | flops 32 | bytes 256 | tf_op jit(solution)/shard_map/while/body/eval_jaxpr/psum | solution.py:40
  581.4 29.0 %psum.49 = f32[1,32]{1,0:T(1,128)S(1)} all-reduce(f32[1,32]{1,0:T(1,128)S(1)} %bitcast.109), channel_id=1, replica_groups=mesh['segment'=8,'rows'=16,'dp'=4] {'rows'}, use_global_device_ids=true, to_apply=%region_6.6 | all-reduce | flops 32 | bytes 256 | tf_op jit(solution)/shard_map/while/body/eval_jaxpr/psum | solution.py:43
  612.7 4.5 collective-permute-start.1
  627.6 29.3 %psum.48 = f32[1,32]{1,0:T(1,128)S(1)} all-reduce(f32[1,32]{1,0:T(1,128)S(1)} %bitcast.110), channel_id=1, replica_groups=mesh['segment'=8,'rows'=16,'dp'=4] {'rows'}, use_global_device_ids=true, to_apply=%region_3.3 | all-reduce | flops 32 | bytes 256 | tf_op jit(solution)/shard_map/while/body/eval_jaxpr/psum | solution.py:40
  658.1 28.2 %psum.49 = f32[1,32]{1,0:T(1,128)S(1)} all-reduce(f32[1,32]{1,0:T(1,128)S(1)} %bitcast.109), channel_id=1, replica_groups=mesh['segment'=8,'rows'=16,'dp'=4] {'rows'}, use_global_device_ids=true, to_apply=%region_6.6 | all-reduce | flops 32 | bytes 256 | tf_op jit(solution)/shard_map/while/body/eval_jaxpr/psum | solution.py:43
  704.9 29.0 %psum.48 = f32[1,32]{1,0:T(1,128)S(1)} all-reduce(f32[1,32]{1,0:T(1,128)S(1)} %bitcast.110), channel_id=1, replica_groups=mesh['segment'=8,'rows'=16,'dp'=4] {'rows'}, use_global_device_ids=true, to_apply=%region_3.3 | all-reduce | flops 32 | bytes 256 | tf_op jit(solution)/shard_map/while/body/eval_jaxpr/psum | solution.py:40
  735.1 28.6 %psum.49 = f32[1,32]{1,0:T(1,128)S(1)} all-reduce(f32[1,32]{1,0:T(1,128)S(1)} %bitcast.109), channel_id=1, replica_groups=mesh['segment'=8,'rows'=16,'dp'=4] {'rows'}, use_global_device_ids=true, to_apply=%region_6.6 | all-reduce | flops 32 | bytes 256 | tf_op jit(solution)/shard_map/while/body/eval_jaxpr/psum | solution.py:43
  783.4 29.0 %psum.48 = f32[1,32]{1,0:T(1,128)S(1)} all-reduce(f32[1,32]{1,0:T(1,128)S(1)} %bitcast.110), channel_id=1, replica_groups=mesh['segment'=8,'rows'=16,'dp'=4] {'rows'}, use_global_device_ids=true, to_apply=%region_3.3 | all-reduce | flops 32 | bytes 256 | tf_op jit(solution)/shard_map/while/body/eval_jaxpr/psum | solution.py:40
  813.6 28.5 %psum.49 = f32[1,32]{1,0:T(1,128)S(1)} all-reduce(f32[1,32]{1,0:T(1,128)S(1)} %bitcast.109), channel_id=1, replica_groups=mesh['segment'=8,'rows'=16,'dp'=4] {'rows'}, use_global_device_ids=true, to_apply=%region_6.6 | all-reduce | flops 32 | bytes 256 | tf_op jit(solution)/shard_map/while/body/eval_jaxpr/psum | solution.py:43
  859.5 82.2 %all-reduce.4.cloned.1.call-done = f32[3456,128]{1,0:T(8,128)} async-done(((f32[3456,128]{1,0:T(8,128)}), f32[3456,128]{1,0:T(8,128)}) %all-reduce.4.cloned.1.call-update) | async-done | bytes 1769488 | tf_op jit(solution)/shard_map/psum | solution.py:125
  941.8 146.1 %all-reduce.6.cloned.1.call-done = f32[3456,128]{1,0:T(8,128)} async-done(((f32[3456,128]{1,0:T(8,128)}), f32[3456,128]{1,0:T(8,128)}) %all-reduce.6.cloned.1.call-update) | async-done | bytes 1769488 | tf_op jit(solution)/shard_map/psum | solution.py:125
  (709 shorter events, 169.1 us)
Async XLA Ops:
  7.2 934.6 %all-reduce.4.cloned.1.call-start = ((), (), s32[]{:S(2)}) async-start(), calls=%async_computation | async-start | bytes 3538944 | tf_op jit(solution)/shard_map/psum | solution.py:125
  76.0 6.5 collective-permute-start
  77.3 5.9 collective-permute-start.1
  85.6 3.6 collective-permute-start.2
  153.8 6.5 collective-permute-start
  155.1 5.9 collective-permute-start.1
  229.8 6.5 collective-permute-start
  231.1 5.9 collective-permute-start.1
  239.3 3.6 collective-permute-start.2
  306.3 6.5 collective-permute-start
  307.6 5.9 collective-permute-start.1
  315.9 3.6 collective-permute-start.2
  382.3 6.5 collective-permute-start
  383.6 5.9 collective-permute-start.1
  391.8 3.6 collective-permute-start.2
  458.9 6.5 collective-permute-start
  460.2 5.9 collective-permute-start.1
  534.8 6.5 collective-permute-start
  536.1 5.9 collective-permute-start.1
  544.3 3.6 collective-permute-start.2
  611.4 6.5 collective-permute-start
  612.7 5.9 collective-permute-start.1
  687.3 6.5 collective-permute-start
  688.6 5.9 collective-permute-start.1
  696.8 5.0 collective-permute-start.2
  764.6 6.5 collective-permute-start
  765.9 5.9 collective-permute-start.1
  774.2 6.1 collective-permute-start.2
  843.0 6.5 collective-permute-start
  844.3 5.9 collective-permute-start.1
  852.6 5.6 collective-permute-start.2
  859.4 228.4 %all-reduce.6.cloned.1.call-start = ((), (), s32[]{:S(2)}) async-start(), calls=%async_computation.1 | async-start | bytes 3538944 | tf_op jit(solution)/shard_map/psum | solution.py:125
  (49 other events, 136.8 us)
Sparse Core Ops, SparseCore 0:
  859.6 82.1 all-reduce.3
  944.2 143.5 all-reduce.5
